TPU v7x, 768 devices: a whole 4x8x12 slice. The times are simulated.
768 devices in a mesh: samp: 24 (over x, z_lo), space: 32 (over z_hi, y, core).
Axes of the slice: x: 4, y: 8, z: 12 (z_hi: 2, z_lo: 6; z = z_hi * 6 + z_lo), core: 2. Of those that a mesh axis runs over, the one named last changes fastest.
Arguments:
- tide_state: float32 [8, 2, 1024, 3072], P(None, None, 'space', 'samp'), may hold values from -6 to 6
- forcing: float32 [8, 2, 1024, 3072], P(None, None, 'space', 'samp'), may hold values from -6 to 6
- wet_mask: int32 [1024, 3072], P('space', 'samp'), may hold values 0 or 1
- depth_band: int32 [1024, 3072], P('space', 'samp'), may hold values from 0 to 7
- drag_table: float32 [8], replicated, may hold values from 0.02 to 0.2
- stiff_table: float32 [8], replicated, may hold values from 0.25 to 2
- sample_times: float32 [48], replicated, may hold values from 0 to 720
- zonal_inverse: float32 [8, 128, 128], replicated, may hold values from -0.5 to 1.5
- meridional_inverse: float32 [8, 512, 512], replicated, may hold values from -0.5 to 1.5
Outputs:
- new_state: float32 [8, 2, 1024, 3072], P(None, None, 'space', 'samp')
All inputs are finite; a program needn't handle non-finite values. No bound on the sum of `wet_mask` on one device may be relied on, other than what follows from the above.
Results may differ from a plain program's by a relative error of at most 0.00013.
Values sent between devices are 32-bit elements; how exact they have to be, the bound alone decides.
A program may use at most 64 MiB of HBM per device.

v0:
```python
import functools

import jax
import jax.numpy as jnp
from jax import lax
from jax.experimental import pallas as pl
from jax.experimental.pallas import tpu as pltpu
from jax.sharding import PartitionSpec as P

MESH = pl.DeviceIdType.MESH
ITERS = 2
ROWS = 32
LANES = 128
COMPS = 16
SAMPLES = 48
RANKS = 16
CHIPS = 8
LM = 512

TIDAL_FREQUENCIES = (
    0.505868,
    0.5235988,
    0.4963657,
    0.5250316,
    0.2625162,
    0.2433523,
    0.2610812,
    0.2338335,
)

OFFSETS = [(dy, dc) for dy in (4, 3, 5, 2, 6, 1, 7) for dc in (0, 1)] + [(0, 1)]


def rotated_cosine(phase, quarter):
    turns = jnp.floor(phase * 0.63661977236758134308 + 0.5)
    rest = phase - turns * 1.5703125
    rest = rest - turns * 4.837512969970703125e-4
    rest = rest - turns * 7.54978995489188216e-8
    quadrant = (turns.astype(jnp.int32) + quarter) & 3
    square = rest * rest
    cosine = 1.0 + square * (
        -0.5 + square * (4.166664568298827e-2 + square * (-1.388731625493765e-3 + square * 2.443315711809948e-5))
    )
    sine = rest + rest * square * (
        -1.6666654611e-1 + square * (8.3321608736e-3 + square * -1.9515295891e-4)
    )
    value = jnp.where((quadrant & 1) == 1, -sine, cosine)
    return jnp.where(quadrant >= 2, -value, value)


def speeds_at(component):
    constituent = component >> 1
    speeds = jnp.zeros(component.shape, jnp.float32)
    for index, speed in enumerate(TIDAL_FREQUENCIES):
        speeds = jnp.where(constituent == index, jnp.float32(speed), speeds)
    return speeds


def high_part(value):
    return value.astype(jnp.bfloat16).astype(jnp.float32)


def split(value):
    high = value.astype(jnp.bfloat16)
    low = (value - high.astype(jnp.float32)).astype(jnp.bfloat16)
    return high, low


def iota(shape, dim):
    return lax.broadcasted_iota(jnp.int32, shape, dim)


def build_factors(times_ref, ahead_ref, back_ref):
    lane = iota((8, LANES), 1)
    row_times = jnp.zeros((8, LANES), jnp.float32)
    ahead_times = jnp.zeros((8, LANES), jnp.float32)
    for t in range(SAMPLES):
        value = times_ref[t]
        row_times = jnp.where((lane == 32 + t) | (lane == 80 + t), value, row_times)
        ahead_times = jnp.where((lane == t) | (lane == 48 + t), value, ahead_times)
    column_times = jnp.transpose(jnp.broadcast_to(ahead_times[0:1], (LANES, LANES)))[:96, :32]
    shape = (96, 32)
    col = iota(shape, 1)
    comp = col & 15
    value = rotated_cosine(column_times * speeds_at(comp), comp & 1)
    high = high_part(value)
    low = jnp.where(col < 16, value - high, 0.0)
    ahead_ref[...] = jnp.where(iota(shape, 0) < 48, high, low).astype(jnp.bfloat16)
    shape = (32, LANES)
    row, col = iota(shape, 0), iota(shape, 1)
    comp = row & 15
    speed = speeds_at(comp)
    times = jnp.broadcast_to(row_times[0:1], shape)
    basis = rotated_cosine(times * speed, comp & 1)
    other = col & 15
    turn = jnp.where(other == (comp ^ 1), jnp.where((comp & 1) == 0, -speed, speed), 0.0)
    value = jnp.where(col < 32, turn, basis)
    high = high_part(value)
    low_used = (col < 16) | ((col >= 32) & (col < 80))
    low = jnp.where(low_used, value - high, 0.0)
    back_ref[...] = jnp.where(row < 16, high, low).astype(jnp.bfloat16)


def kernel(
    tide_hbm, forcing_hbm, wet_hbm, band_hbm, drag_ref, stiff_ref, times_ref, zonal_hbm, meridional_hbm,
    out_ref,
    tide, forcing, wet_int, band, zonal_raw, mer_raw,
    wet, drag, stiff, ahead, back, zonal_w, mer_high, mer_low,
    cur, mix, back_terms, terms, edge_out, edge_in, row_in,
    fwd_out, fwd_in, ret_out, ret_in,
    local_sem, halo_send, halo_recv, fwd_send, fwd_recv, ret_send, ret_recv,
):
    samp = lax.axis_index("samp")
    space = lax.axis_index("space")
    n_samp = lax.axis_size("samp")
    n_space = lax.axis_size("space")
    rank = space % RANKS
    base = space - rank
    chip, core = rank // 2, rank % 2
    owned = rank // 2

    loads = [
        pltpu.make_async_copy(wet_hbm, wet_int, local_sem.at[0]),
        pltpu.make_async_copy(band_hbm, band, local_sem.at[1]),
        pltpu.make_async_copy(tide_hbm, tide, local_sem.at[2]),
        pltpu.make_async_copy(forcing_hbm, forcing, local_sem.at[3]),
        pltpu.make_async_copy(zonal_hbm.at[owned], zonal_raw, local_sem.at[4]),
        pltpu.make_async_copy(meridional_hbm.at[owned], mer_raw, local_sem.at[5]),
    ]
    for load in loads:
        load.start()

    north = {"space": (space + n_space - 1) % n_space}
    south = {"space": (space + 1) % n_space}
    west = {"samp": (samp + n_samp - 1) % n_samp}
    east = {"samp": (samp + 1) % n_samp}

    peers = []
    for dy, dc in OFFSETS:
        peers.append(((chip + dy) % CHIPS) * 2 + (core + dc) % 2)

    barrier = pltpu.get_barrier_semaphore()
    for target in [north, south, west, east] + [{"space": base + peer} for peer in peers]:
        pl.semaphore_signal(barrier, inc=1, device_id=target, device_id_type=MESH)

    build_factors(times_ref, ahead, back)

    loads[0].wait()
    loads[1].wait()
    wet[...] = wet_int[...].astype(jnp.float32)
    drags = jnp.zeros((ROWS, LANES), jnp.float32)
    stiffs = jnp.zeros((ROWS, LANES), jnp.float32)
    for level in range(drag_ref.shape[0]):
        here = band[...] == level
        drags = jnp.where(here, drag_ref[level], drags)
        stiffs = jnp.where(here, stiff_ref[level], stiffs)
    drag[...] = drags * (2.0 / SAMPLES)
    stiff[...] = stiffs

    tile = (COMPS, LANES)
    lane = iota(tile, 1)
    has_north = (space > 0).astype(jnp.float32)
    has_south = (space < n_space - 1).astype(jnp.float32)

    def shift(value, amount):
        amount = amount % LANES
        return value if amount == 0 else pltpu.roll(value, amount, 1)

    def set_state(it, r, value, edges):
        cur[it, comps(r), :] = value
        high, low = split(value)
        cols = pl.ds(r * LANES, LANES)
        mix[0:16, cols] = high
        mix[16:32, cols] = low
        first, last = edges
        first = jnp.where(lane == r, shift(value, r), first)
        last = jnp.where(lane == r, shift(value, r + 1), last)
        return first, last

    def comps(r):
        return pl.ds(r * COMPS, COMPS)

    def spread(ref, r):
        return jnp.broadcast_to(ref[pl.ds(r, 1), :], tile)

    def piece(rank_index):
        return pl.ds(pl.multiple_of(rank_index * ROWS, ROWS), ROWS)

    def exchange(it, source, target, send, recv):
        copies = []
        for peer in peers:
            copy = pltpu.make_async_remote_copy(
                src_ref=source.at[it, piece(peer), :],
                dst_ref=target.at[it, piece(rank), :],
                send_sem=send.at[it, peer],
                recv_sem=recv.at[it, rank],
                device_id={"space": base + peer},
                device_id_type=MESH,
            )
            copy.start()
            copies.append(copy)
        return copies

    def arrival(it, peer, source, target, send, recv):
        return pltpu.make_async_remote_copy(
            src_ref=source.at[it, piece(rank), :],
            dst_ref=target.at[it, piece(peer), :],
            send_sem=send.at[it, peer],
            recv_sem=recv.at[it, peer],
            device_id={"space": base + peer},
            device_id_type=MESH,
        )

    pending = []
    for it in range(ITERS):
        edges = (jnp.zeros(tile, jnp.float32), jnp.zeros(tile, jnp.float32))
        if it == 0:
            loads[2].wait()
            for r in range(ROWS):
                value = spread(wet, r) * tide[pl.ds(r, COMPS, stride=ROWS), :]
                edges = set_state(it, r, value, edges)
        else:
            for r in range(ROWS):
                step = ret_in[it - 1, pl.ds(r, COMPS, stride=ROWS), :]
                value = cur[it - 1, comps(r), :] + 0.25 * spread(wet, r) * step
                edges = set_state(it, r, value, edges)
        edge_out[it, 0] = edges[0]
        edge_out[it, 1] = edges[1]
        if it == 0:
            pl.semaphore_wait(barrier, 4 + len(peers))
        halos = []
        for slot, source, target, device in (
            (0, cur.at[it, comps(ROWS - 1), :], row_in.at[it, 0], south),
            (1, cur.at[it, comps(0), :], row_in.at[it, 1], north),
            (2, edge_out.at[it, 1], edge_in.at[it, 0], east),
            (3, edge_out.at[it, 0], edge_in.at[it, 1], west),
        ):
            copy = pltpu.make_async_remote_copy(
                src_ref=source,
                dst_ref=target,
                send_sem=halo_send.at[it, slot],
                recv_sem=halo_recv.at[it, slot],
                device_id=device,
                device_id_type=MESH,
            )
            copy.start()
            halos.append(copy)

        for start in range(0, ROWS, 4):
            cols = pl.ds(start * LANES, 4 * LANES)
            both = jnp.dot(ahead[...], mix[0:32, cols], preferred_element_type=jnp.float32)
            velocity = both[:SAMPLES] + both[SAMPLES:]
            for q in range(4):
                r = start + q
                part = velocity[:, q * LANES:(q + 1) * LANES]
                stress = jnp.broadcast_to(drag[pl.ds(r, 1), :], part.shape) * jnp.abs(part) * part
                high, low = split(stress)
                mix[32:80, pl.ds(r * LANES, LANES)] = high
                mix[80:128, pl.ds(r * LANES, LANES)] = low
            both = jnp.dot(back[...], mix[:, cols], preferred_element_type=jnp.float32)
            back_terms[:, cols] = both[:COMPS] + both[COMPS:]

        for copy in halos:
            copy.wait_recv()
        pending.extend(halos)
        west_in, east_in = edge_in[it, 0], edge_in[it, 1]
        for r in range(ROWS):
            value = cur[it, comps(r), :]
            up = cur[it, comps(r - 1), :] if r > 0 else row_in[it, 0] * has_north
            down = cur[it, comps(r + 1), :] if r < ROWS - 1 else row_in[it, 1] * has_south
            left = jnp.where(lane == 0, shift(west_in, LANES - r), shift(value, 1))
            right = jnp.where(lane == LANES - 1, shift(east_in, LANES - 1 - r), shift(value, LANES - 1))
            neighbours = (up + down) + (left + right)
            total = value + back_terms[:, pl.ds(r * LANES, LANES)] + spread(stiff, r) * (4.0 * value - neighbours)
            terms[comps(r), :] = total
        for c in range(COMPS):
            rows = pl.ds(c * ROWS, ROWS)
            fallen = terms[pl.ds(c, ROWS, stride=COMPS), :]
            if it == 0 and c == 0:
                loads[3].wait()
            fwd_out[it, rows, :] = wet[...] * (forcing[rows, :] - fallen)
        pending.extend(exchange(it, fwd_out, fwd_in, fwd_send, fwd_recv))
        fwd_in[it, piece(rank), :] = fwd_out[it, piece(rank), :]

        if it == 0:
            loads[4].wait()
            loads[5].wait()
            high, low = split(jnp.transpose(zonal_raw[...]))
            zonal_w[0:128, 0:128] = high
            zonal_w[0:128, 128:256] = low
            zonal_w[128:256, 0:128] = high
            zonal_w[128:256, 128:256] = jnp.zeros((LANES, LANES), jnp.bfloat16)
            for start in range(0, LM, 64):
                high, low = split(mer_raw[start:start + 64, :])
                mer_high[start:start + 64, :] = high
                mer_low[start:start + 64, :] = low

        for peer in peers:
            arrival(it, peer, fwd_out, fwd_in, fwd_send, fwd_recv).wait_recv()
        high, low = split(fwd_in[it])
        both = jnp.dot(jnp.concatenate([high, low], axis=1), zonal_w[...], preferred_element_type=jnp.float32)
        high, low = split(both[:, :LANES] + both[:, LANES:])
        both = jnp.dot(mer_high[...], jnp.concatenate([high, low], axis=1), preferred_element_type=jnp.float32)
        third = jnp.dot(mer_low[...], high, preferred_element_type=jnp.float32)
        ret_out[it] = both[:, :LANES] + both[:, LANES:] + third
        pending.extend(exchange(it, ret_out, ret_in, ret_send, ret_recv))
        ret_in[it, piece(rank), :] = ret_out[it, piece(rank), :]
        for peer in peers:
            arrival(it, peer, ret_out, ret_in, ret_send, ret_recv).wait_recv()

    last = ITERS - 1
    for c in range(COMPS):
        rows = pl.ds(c * ROWS, ROWS)
        state = cur[last, pl.ds(c, ROWS, stride=COMPS), :]
        out_ref[rows, :] = state + 0.25 * wet[...] * ret_in[last, rows, :]
    for copy in pending:
        copy.wait_send()


def body(
    tide_state,
    forcing,
    wet_mask,
    depth_band,
    drag_table,
    stiff_table,
    sample_times,
    zonal_inverse,
    meridional_inverse,
):
    flat = (COMPS * ROWS, LANES)
    f32, bf16 = jnp.float32, jnp.bfloat16
    dma = pltpu.SemaphoreType.DMA
    any_spec = pl.BlockSpec(memory_space=pl.ANY)
    smem = pl.BlockSpec(memory_space=pltpu.SMEM)
    result = pl.pallas_call(
        kernel,
        out_shape=jax.ShapeDtypeStruct(flat, f32),
        in_specs=[any_spec] * 4 + [smem] * 3 + [any_spec] * 2,
        out_specs=pl.BlockSpec(memory_space=pltpu.VMEM),
        scratch_shapes=[
            pltpu.VMEM(flat, f32),
            pltpu.VMEM(flat, f32),
            pltpu.VMEM((ROWS, LANES), jnp.int32),
            pltpu.VMEM((ROWS, LANES), jnp.int32),
            pltpu.VMEM((LANES, LANES), f32),
            pltpu.VMEM((LM, LM), f32),
            pltpu.VMEM((ROWS, LANES), f32),
            pltpu.VMEM((ROWS, LANES), f32),
            pltpu.VMEM((ROWS, LANES), f32),
            pltpu.VMEM((96, 32), bf16),
            pltpu.VMEM((32, LANES), bf16),
            pltpu.VMEM((256, 256), bf16),
            pltpu.VMEM((LM, LM), bf16),
            pltpu.VMEM((LM, LM), bf16),
            pltpu.VMEM((ITERS,) + flat, f32),
            pltpu.VMEM((LANES, ROWS * LANES), bf16),
            pltpu.VMEM((COMPS, ROWS * LANES), f32),
            pltpu.VMEM(flat, f32),
            pltpu.VMEM((ITERS, 2, COMPS, LANES), f32),
            pltpu.VMEM((ITERS, 2, COMPS, LANES), f32),
            pltpu.VMEM((ITERS, 2, COMPS, LANES), f32),
            pltpu.VMEM((ITERS,) + flat, f32),
            pltpu.VMEM((ITERS,) + flat, f32),
            pltpu.VMEM((ITERS,) + flat, f32),
            pltpu.VMEM((ITERS,) + flat, f32),
            dma((6,)),
            dma((ITERS, 4)),
            dma((ITERS, 4)),
            dma((ITERS, RANKS)),
            dma((ITERS, RANKS)),
            dma((ITERS, RANKS)),
            dma((ITERS, RANKS)),
        ],
        compiler_params=pltpu.CompilerParams(
            collective_id=0, has_side_effects=True, vmem_limit_bytes=40 * 1024 * 1024
        ),
        cost_estimate=pl.CostEstimate(flops=600000000, bytes_accessed=2500000, transcendentals=0),
    )(
        tide_state.reshape(flat),
        forcing.reshape(flat),
        wet_mask,
        depth_band,
        drag_table,
        stiff_table,
        sample_times,
        zonal_inverse,
        meridional_inverse,
    )
    return result.reshape(tide_state.shape)


def solution(mesh):
    grid = P(None, None, "space", "samp")
    return jax.shard_map(
        body,
        mesh=mesh,
        in_specs=(grid, grid, P("space", "samp"), P("space", "samp"), P(), P(), P(), P(), P()),
        out_specs=grid,
        check_vma=False,
    )
```

profile of v0, /device:TPU:1, one launch (start us, length us, event | category | flops | bytes accessed | tf_op | source)
XLA Modules:
  0.0 75.3 jit_solution(9194101284119622988)
XLA Ops:
  0.0 0.0 copy-start
  0.0 3.4 %copy-done = f32[8,512,512]{2,1,0:T(8,128)S(1)} copy-done((f32[8,512,512]{2,1,0:T(8,128)S(1)}, f32[8,512,512]{2,1,0:T(8,128)}, u32[]{:S(2)}) %copy-start) | copy-done | bytes 8388632
  3.4 0.0 copy-start.1
  3.4 1.0 %copy-done.1 = f32[8,128,128]{2,1,0:T(8,128)S(1)} copy-done((f32[8,128,128]{2,1,0:T(8,128)S(1)}, f32[8,128,128]{2,1,0:T(8,128)}, u32[]{:S(2)}) %copy-start.1) | copy-done | bytes 524312
  4.4 0.0 copy-start.2
  4.4 0.9 %copy-done.2 = f32[8,2,32,128]{3,2,1,0:T(8,128)S(1)} copy-done((f32[8,2,32,128]{3,2,1,0:T(8,128)S(1)}, f32[8,2,32,128]{3,2,1,0:T(8,128)}, u32[]{:S(2)}) %copy-start.2) | copy-done | bytes 262168
  5.4 0.0 copy-start.3
  5.4 0.9 %copy-done.3 = f32[8,2,32,128]{3,2,1,0:T(8,128)S(1)} copy-done((f32[8,2,32,128]{3,2,1,0:T(8,128)S(1)}, f32[8,2,32,128]{3,2,1,0:T(8,128)}, u32[]{:S(2)}) %copy-start.3) | copy-done | bytes 262168
  6.3 0.0 copy-start.4
  6.3 0.7 copy-done.4
  7.0 0.0 copy-start.5
  7.0 0.7 copy-done.5
  7.8 0.0 copy-start.6
  7.8 0.7 copy-done.6
  8.4 0.0 copy-start.7
  8.4 0.7 copy-done.7
  9.1 0.0 copy-start.8
  9.1 0.7 copy-done.8
  9.7 64.9 %shard_map.91 = f32[512,128]{1,0:T(8,128)S(1)} custom-call(f32[512,128]{1,0:T(8,128)S(1)} %bitcast.4, f32[512,128]{1,0:T(8,128)S(1)} %bitcast.5, s32[32,128]{1,0:T(8,128)S(1)} %copy-done.4, s32[32,128]{1,0:T(8,128)S(1)} %copy-done.5, f32[8]{0:T(128)S(1)} %copy-done.6, f32[8]{0:T(128)S(1)} %copy-done.7, f32[48]{0:T(128)S(1)} %copy-done.8, ...), custom_call_target="tpu_custom_call" | custom-call | flops 600000000 | bytes 2500000 | tf_op jit(solution)/shard_map/pallas_call | solution.py:336
  74.6 0.7 copy.11
Async XLA Ops:
  0.0 3.4 %copy-start = (f32[8,512,512]{2,1,0:T(8,128)S(1)}, f32[8,512,512]{2,1,0:T(8,128)}, u32[]{:S(2)}) copy-start(f32[8,512,512]{2,1,0:T(8,128)} %meridional_hbm.1) | copy-start | bytes 25165828
  3.4 1.0 %copy-start.1 = (f32[8,128,128]{2,1,0:T(8,128)S(1)}, f32[8,128,128]{2,1,0:T(8,128)}, u32[]{:S(2)}) copy-start(f32[8,128,128]{2,1,0:T(8,128)} %zonal_hbm.1) | copy-start | bytes 1572868
  4.4 0.9 %copy-start.2 = (f32[8,2,32,128]{3,2,1,0:T(8,128)S(1)}, f32[8,2,32,128]{3,2,1,0:T(8,128)}, u32[]{:S(2)}) copy-start(f32[8,2,32,128]{3,2,1,0:T(8,128)} %param.9) | copy-start | bytes 786436
  5.4 0.9 %copy-start.3 = (f32[8,2,32,128]{3,2,1,0:T(8,128)S(1)}, f32[8,2,32,128]{3,2,1,0:T(8,128)}, u32[]{:S(2)}) copy-start(f32[8,2,32,128]{3,2,1,0:T(8,128)} %param.10) | copy-start | bytes 786436
  6.3 0.7 copy-start.4
  7.0 0.7 copy-start.5
  7.8 0.7 copy-start.6
  8.4 0.7 copy-start.7
  9.1 0.7 copy-start.8
where the time goes:
time: 75.7 us; the launch traced here: 75.3 us
  Pallas kernels  64.9 us (86%)
  local copies, waits for them, and re-layouts  10.4 us (14%)
    pallas_call x1, Pallas kernels, body(): pl.pallas_call(kernel, out_shape=jax.ShapeDtypeStruct(flat, f32), in_spec...  64.9 us
    unnamed x19, local copies, waits for them, and re-layouts  10.4 us

commit v1 on v0

--- a/solution.py
+++ b/solution.py
@@ -211,24 +211,7 @@
             device_id_type=MESH,
         )
 
-    pending = []
-    for it in range(ITERS):
-        edges = (jnp.zeros(tile, jnp.float32), jnp.zeros(tile, jnp.float32))
-        if it == 0:
-            loads[2].wait()
-            for r in range(ROWS):
-                value = spread(wet, r) * tide[pl.ds(r, COMPS, stride=ROWS), :]
-                edges = set_state(it, r, value, edges)
-        else:
-            for r in range(ROWS):
-                step = ret_in[it - 1, pl.ds(r, COMPS, stride=ROWS), :]
-                value = cur[it - 1, comps(r), :] + 0.25 * spread(wet, r) * step
-                edges = set_state(it, r, value, edges)
-        edge_out[it, 0] = edges[0]
-        edge_out[it, 1] = edges[1]
-        if it == 0:
-            pl.semaphore_wait(barrier, 4 + len(peers))
-        halos = []
+    def send_halos(it, halos):
         for slot, source, target, device in (
             (0, cur.at[it, comps(ROWS - 1), :], row_in.at[it, 0], south),
             (1, cur.at[it, comps(0), :], row_in.at[it, 1], north),
@@ -246,6 +229,24 @@
             copy.start()
             halos.append(copy)
 
+    pending = []
+    for it in range(ITERS):
+        edges = (jnp.zeros(tile, jnp.float32), jnp.zeros(tile, jnp.float32))
+        if it == 0:
+            loads[2].wait()
+            for r in range(ROWS):
+                value = spread(wet, r) * tide[pl.ds(r, COMPS, stride=ROWS), :]
+                edges = set_state(it, r, value, edges)
+        else:
+            for r in range(ROWS):
+                step = ret_in[it - 1, pl.ds(r, COMPS, stride=ROWS), :]
+                value = cur[it - 1, comps(r), :] + 0.25 * spread(wet, r) * step
+                edges = set_state(it, r, value, edges)
+        edge_out[it, 0] = edges[0]
+        edge_out[it, 1] = edges[1]
+        halos = []
+        if it > 0:
+            send_halos(it, halos)
         for start in range(0, ROWS, 4):
             cols = pl.ds(start * LANES, 4 * LANES)
             both = jnp.dot(ahead[...], mix[0:32, cols], preferred_element_type=jnp.float32)
@@ -260,6 +261,9 @@
             both = jnp.dot(back[...], mix[:, cols], preferred_element_type=jnp.float32)
             back_terms[:, cols] = both[:COMPS] + both[COMPS:]
 
+        if it == 0:
+            pl.semaphore_wait(barrier, 4 + len(peers))
+            send_halos(it, halos)
         for copy in halos:
             copy.wait_recv()
         pending.extend(halos)
@@ -331,7 +335,7 @@
     flat = (COMPS * ROWS, LANES)
     f32, bf16 = jnp.float32, jnp.bfloat16
     dma = pltpu.SemaphoreType.DMA
-    any_spec = pl.BlockSpec(memory_space=pl.ANY)
+    any_spec = pl.BlockSpec(memory_space=pltpu.HBM)
     smem = pl.BlockSpec(memory_space=pltpu.SMEM)
     result = pl.pallas_call(
         kernel,
@@ -373,7 +377,7 @@
             dma((ITERS, RANKS)),
         ],
         compiler_params=pltpu.CompilerParams(
-            collective_id=0, has_side_effects=True, vmem_limit_bytes=40 * 1024 * 1024
+            collective_id=0, has_side_effects=True, vmem_limit_bytes=64 * 1024 * 1024
         ),
         cost_estimate=pl.CostEstimate(flops=600000000, bytes_accessed=2500000, transcendentals=0),
     )(

time: 75.7 us -> 67.2 us (0.89)
  local copies, waits for them, and re-layouts: 10.4 us -> 1.67 us
    unnamed x19 -> x1, local copies, waits for them, and re-layouts: 10.4 us -> 1.67 us
where the time goes in v1:
time: 67.2 us; the launch traced here: 67 us
  Pallas kernels  65.3 us (97%)
  local copies, waits for them, and re-layouts  1.67 us (2%)
    pallas_call x1, Pallas kernels, body(): pl.pallas_call(kernel, out_shape=jax.ShapeDtypeStruct(flat, f32), in_spec...  65.3 us
    unnamed x1, local copies, waits for them, and re-layouts  1.67 us

profile of v1, /device:TPU:1, one launch (start us, length us, event | category | flops | bytes accessed | tf_op | source)
XLA Modules:
  0.0 67.0 jit_solution(11688817973578458006)
XLA Ops:
  0.0 65.3 %shard_map.91 = f32[512,128]{1,0:T(8,128)} custom-call(f32[512,128]{1,0:T(8,128)} %bitcast.4, f32[512,128]{1,0:T(8,128)} %bitcast.5, s32[32,128]{1,0:T(8,128)} %wet_hbm.1, s32[32,128]{1,0:T(8,128)} %band_hbm.1, f32[8]{0:T(128)} %drag_ref.1, f32[8]{0:T(128)} %stiff_ref.1, f32[48]{0:T(128)} %times_ref.1, f32[8,128,128]{2,1,0:T(8,128)} %zonal_hbm.1, ...), custom_call_target="tpu_custom_call" | custom-call | flops 600000000 | bytes 2500000 | tf_op jit(solution)/shard_map/pallas_call | solution.py:340
  65.3 1.7 %copy.11 = f32[8,2,32,128]{3,2,1,0:T(8,128)} copy(f32[8,2,32,128]{3,2,1,0:T(8,128)} %bitcast.3) | data formatting | bytes 524288

commit v2 on v1

--- a/solution.py
+++ b/solution.py
@@ -106,9 +106,9 @@
     out_ref,
     tide, forcing, wet_int, band, zonal_raw, mer_raw,
     wet, drag, stiff, ahead, back, zonal_w, mer_high, mer_low,
-    cur, mix, back_terms, terms, edge_out, edge_in, row_in,
+    cur, mix, back_terms, terms, halo_out, halo_in, fix_out, fix_in, fix, end_out, end_in, zonal_lhs,
     fwd_out, fwd_in, ret_out, ret_in,
-    local_sem, halo_send, halo_recv, fwd_send, fwd_recv, ret_send, ret_recv,
+    local_sem, halo_send, halo_recv, fix_send, fix_recv, end_send, end_recv, fwd_send, fwd_recv, ret_send, ret_recv,
 ):
     samp = lax.axis_index("samp")
     space = lax.axis_index("space")
@@ -134,13 +134,14 @@
     south = {"space": (space + 1) % n_space}
     west = {"samp": (samp + n_samp - 1) % n_samp}
     east = {"samp": (samp + 1) % n_samp}
+    across = {"space": (space + RANKS) % n_space}
 
     peers = []
     for dy, dc in OFFSETS:
         peers.append(((chip + dy) % CHIPS) * 2 + (core + dc) % 2)
 
     barrier = pltpu.get_barrier_semaphore()
-    for target in [north, south, west, east] + [{"space": base + peer} for peer in peers]:
+    for target in [north, south, west, east, across] + [{"space": base + peer} for peer in peers]:
         pl.semaphore_signal(barrier, inc=1, device_id=target, device_id_type=MESH)
 
     build_factors(times_ref, ahead, back)
@@ -159,6 +160,8 @@
 
     tile = (COMPS, LANES)
     lane = iota(tile, 1)
+    block = (ROWS, LANES)
+    block_row, block_lane = iota(block, 0), iota(block, 1)
     has_north = (space > 0).astype(jnp.float32)
     has_south = (space < n_space - 1).astype(jnp.float32)
 
@@ -166,87 +169,50 @@
         amount = amount % LANES
         return value if amount == 0 else pltpu.roll(value, amount, 1)
 
-    def set_state(it, r, value, edges):
+    def comps(r):
+        return pl.ds(r * COMPS, COMPS)
+
+    def spread(ref, r):
+        return jnp.broadcast_to(ref[pl.ds(r, 1), :], tile)
+
+    def piece(rank_index, rows=ROWS):
+        return pl.ds(pl.multiple_of(rank_index * rows, rows), rows)
+
+    def columns_to_lanes(value, first_lane):
+        picked = jnp.where(block_lane == block_row + first_lane, jnp.broadcast_to(value, block), 0.0)
+        return picked
+
+    def set_state(it, r, value):
         cur[it, comps(r), :] = value
         high, low = split(value)
         cols = pl.ds(r * LANES, LANES)
         mix[0:16, cols] = high
         mix[16:32, cols] = low
-        first, last = edges
-        first = jnp.where(lane == r, shift(value, r), first)
-        last = jnp.where(lane == r, shift(value, r + 1), last)
-        return first, last
-
-    def comps(r):
-        return pl.ds(r * COMPS, COMPS)
-
-    def spread(ref, r):
-        return jnp.broadcast_to(ref[pl.ds(r, 1), :], tile)
-
-    def piece(rank_index):
-        return pl.ds(pl.multiple_of(rank_index * ROWS, ROWS), ROWS)
-
-    def exchange(it, source, target, send, recv):
+
+    def remote(source, target, send, recv, device):
+        return pltpu.make_async_remote_copy(
+            src_ref=source, dst_ref=target, send_sem=send, recv_sem=recv, device_id=device, device_id_type=MESH
+        )
+
+    def exchange(source, target, send, recv, rows):
         copies = []
         for peer in peers:
-            copy = pltpu.make_async_remote_copy(
-                src_ref=source.at[it, piece(peer), :],
-                dst_ref=target.at[it, piece(rank), :],
-                send_sem=send.at[it, peer],
-                recv_sem=recv.at[it, rank],
-                device_id={"space": base + peer},
-                device_id_type=MESH,
+            copy = remote(
+                source.at[piece(peer, rows), :], target.at[piece(rank, rows), :], send.at[peer], recv.at[rank],
+                {"space": base + peer},
             )
             copy.start()
             copies.append(copy)
+        target[piece(rank, rows), :] = source[piece(rank, rows), :]
         return copies
 
-    def arrival(it, peer, source, target, send, recv):
-        return pltpu.make_async_remote_copy(
-            src_ref=source.at[it, piece(rank), :],
-            dst_ref=target.at[it, piece(peer), :],
-            send_sem=send.at[it, peer],
-            recv_sem=recv.at[it, peer],
-            device_id={"space": base + peer},
-            device_id_type=MESH,
-        )
-
-    def send_halos(it, halos):
-        for slot, source, target, device in (
-            (0, cur.at[it, comps(ROWS - 1), :], row_in.at[it, 0], south),
-            (1, cur.at[it, comps(0), :], row_in.at[it, 1], north),
-            (2, edge_out.at[it, 1], edge_in.at[it, 0], east),
-            (3, edge_out.at[it, 0], edge_in.at[it, 1], west),
-        ):
-            copy = pltpu.make_async_remote_copy(
-                src_ref=source,
-                dst_ref=target,
-                send_sem=halo_send.at[it, slot],
-                recv_sem=halo_recv.at[it, slot],
-                device_id=device,
-                device_id_type=MESH,
-            )
-            copy.start()
-            halos.append(copy)
-
-    pending = []
-    for it in range(ITERS):
-        edges = (jnp.zeros(tile, jnp.float32), jnp.zeros(tile, jnp.float32))
-        if it == 0:
-            loads[2].wait()
-            for r in range(ROWS):
-                value = spread(wet, r) * tide[pl.ds(r, COMPS, stride=ROWS), :]
-                edges = set_state(it, r, value, edges)
-        else:
-            for r in range(ROWS):
-                step = ret_in[it - 1, pl.ds(r, COMPS, stride=ROWS), :]
-                value = cur[it - 1, comps(r), :] + 0.25 * spread(wet, r) * step
-                edges = set_state(it, r, value, edges)
-        edge_out[it, 0] = edges[0]
-        edge_out[it, 1] = edges[1]
-        halos = []
-        if it > 0:
-            send_halos(it, halos)
+    def await_piece(peer, source, target, send, recv, rows):
+        remote(
+            source.at[piece(rank, rows), :], target.at[piece(peer, rows), :], send.at[peer], recv.at[peer],
+            {"space": base + peer},
+        ).wait_recv()
+
+    def friction():
         for start in range(0, ROWS, 4):
             cols = pl.ds(start * LANES, 4 * LANES)
             both = jnp.dot(ahead[...], mix[0:32, cols], preferred_element_type=jnp.float32)
@@ -261,62 +227,172 @@
             both = jnp.dot(back[...], mix[:, cols], preferred_element_type=jnp.float32)
             back_terms[:, cols] = both[:COMPS] + both[COMPS:]
 
-        if it == 0:
-            pl.semaphore_wait(barrier, 4 + len(peers))
-            send_halos(it, halos)
-        for copy in halos:
-            copy.wait_recv()
-        pending.extend(halos)
-        west_in, east_in = edge_in[it, 0], edge_in[it, 1]
+    def local_residual(it):
         for r in range(ROWS):
             value = cur[it, comps(r), :]
-            up = cur[it, comps(r - 1), :] if r > 0 else row_in[it, 0] * has_north
-            down = cur[it, comps(r + 1), :] if r < ROWS - 1 else row_in[it, 1] * has_south
-            left = jnp.where(lane == 0, shift(west_in, LANES - r), shift(value, 1))
-            right = jnp.where(lane == LANES - 1, shift(east_in, LANES - 1 - r), shift(value, LANES - 1))
-            neighbours = (up + down) + (left + right)
+            left = jnp.where(lane == 0, 0.0, shift(value, 1))
+            right = jnp.where(lane == LANES - 1, 0.0, shift(value, LANES - 1))
+            neighbours = left + right
+            if r > 0:
+                neighbours = neighbours + cur[it, comps(r - 1), :]
+            if r < ROWS - 1:
+                neighbours = neighbours + cur[it, comps(r + 1), :]
             total = value + back_terms[:, pl.ds(r * LANES, LANES)] + spread(stiff, r) * (4.0 * value - neighbours)
             terms[comps(r), :] = total
+        if it == 0:
+            loads[3].wait()
         for c in range(COMPS):
             rows = pl.ds(c * ROWS, ROWS)
             fallen = terms[pl.ds(c, ROWS, stride=COMPS), :]
-            if it == 0 and c == 0:
-                loads[3].wait()
             fwd_out[it, rows, :] = wet[...] * (forcing[rows, :] - fallen)
-        pending.extend(exchange(it, fwd_out, fwd_in, fwd_send, fwd_recv))
-        fwd_in[it, piece(rank), :] = fwd_out[it, piece(rank), :]
-
-        if it == 0:
-            loads[4].wait()
-            loads[5].wait()
-            high, low = split(jnp.transpose(zonal_raw[...]))
-            zonal_w[0:128, 0:128] = high
-            zonal_w[0:128, 128:256] = low
-            zonal_w[128:256, 0:128] = high
-            zonal_w[128:256, 128:256] = jnp.zeros((LANES, LANES), jnp.bfloat16)
-            for start in range(0, LM, 64):
-                high, low = split(mer_raw[start:start + 64, :])
-                mer_high[start:start + 64, :] = high
-                mer_low[start:start + 64, :] = low
-
-        for peer in peers:
-            arrival(it, peer, fwd_out, fwd_in, fwd_send, fwd_recv).wait_recv()
-        high, low = split(fwd_in[it])
-        both = jnp.dot(jnp.concatenate([high, low], axis=1), zonal_w[...], preferred_element_type=jnp.float32)
+
+    def edge_terms(owner, it):
+        value = fwd_in[it, piece(owner), :]
+        west_row = jnp.broadcast_to(fix[pl.ds(owner, 1), :], block)
+        east_row = jnp.broadcast_to(fix[pl.ds(owner + RANKS, 1), :], block)
+        north_row = jnp.broadcast_to(fix[pl.ds(owner + 2 * RANKS, 1), :], block)
+        south_row = jnp.broadcast_to(fix[pl.ds(owner + 3 * RANKS, 1), :], block)
+        same = block_lane == block_row
+        west_col = jnp.sum(jnp.where(same, west_row, 0.0), axis=1, keepdims=True)
+        east_col = jnp.sum(jnp.where(same, east_row, 0.0), axis=1, keepdims=True)
+        value = value + jnp.where(block_lane == 0, west_col, 0.0) + jnp.where(block_lane == LANES - 1, east_col, 0.0)
+        value = value + jnp.where(block_row == 0, north_row, 0.0) + jnp.where(block_row == ROWS - 1, south_row, 0.0)
+        high, low = split(value)
+        zonal_lhs[piece(owner), 0:LANES] = high
+        zonal_lhs[piece(owner), LANES:2 * LANES] = low
+
+    def solve(it):
+        both = jnp.dot(zonal_lhs[...], zonal_w[...], preferred_element_type=jnp.float32)
         high, low = split(both[:, :LANES] + both[:, LANES:])
         both = jnp.dot(mer_high[...], jnp.concatenate([high, low], axis=1), preferred_element_type=jnp.float32)
         third = jnp.dot(mer_low[...], high, preferred_element_type=jnp.float32)
         ret_out[it] = both[:, :LANES] + both[:, LANES:] + third
-        pending.extend(exchange(it, ret_out, ret_in, ret_send, ret_recv))
-        ret_in[it, piece(rank), :] = ret_out[it, piece(rank), :]
-        for peer in peers:
-            arrival(it, peer, ret_out, ret_in, ret_send, ret_recv).wait_recv()
-
-    last = ITERS - 1
+
+    pending = []
+    loads[2].wait()
+    first = jnp.zeros(tile, jnp.float32)
+    last = jnp.zeros(tile, jnp.float32)
+    for r in range(ROWS):
+        value = spread(wet, r) * tide[pl.ds(r, COMPS, stride=ROWS), :]
+        set_state(0, r, value)
+        first = jnp.where(lane == r, shift(value, r), first)
+        last = jnp.where(lane == r, shift(value, r + 1), last)
+    wets = wet[...]
+    strength = wets * stiff[...]
+    packed = jnp.sum(
+        columns_to_lanes(wets[:, 0:1], 0)
+        + columns_to_lanes(wets[:, LANES - 1:LANES], 32)
+        + columns_to_lanes(strength[:, 0:1], 64)
+        + columns_to_lanes(strength[:, LANES - 1:LANES], 96),
+        axis=0,
+        keepdims=True,
+    )
+    for slot, value, extra in (
+        (0, cur[0, comps(ROWS - 1), :], wets[ROWS - 1:ROWS]),
+        (1, cur[0, comps(0), :], wets[0:1]),
+        (2, last, shift(packed, LANES - 32)),
+        (3, first, packed),
+    ):
+        halo_out[slot, 0:COMPS, :] = value
+        halo_out[slot, COMPS:COMPS + 8, :] = jnp.broadcast_to(extra, (8, LANES))
+    friction()
+    pl.semaphore_wait(barrier, 5 + len(peers))
+    halos = []
+    for slot, device in ((2, east), (3, west), (0, south), (1, north)):
+        copy = remote(halo_out.at[slot], halo_in.at[slot], halo_send.at[slot], halo_recv.at[slot], device)
+        copy.start()
+        halos.append(copy)
+    pending.extend(halos)
+    local_residual(0)
+    fwd = (fwd_out.at[0], fwd_in.at[0], fwd_send.at[0], fwd_recv.at[0], ROWS)
+    pending.extend(exchange(*fwd))
+
+    for copy in halos:
+        copy.wait_recv()
+    sides = (
+        (2, shift(packed, 64)),
+        (3, shift(packed, 32)),
+        (0, strength[0:1] * has_north),
+        (1, strength[ROWS - 1:ROWS] * has_south),
+    )
+    for j, (slot, factor) in enumerate(sides):
+        factors = jnp.broadcast_to(factor, tile)
+        near = jnp.broadcast_to(halo_in[slot, COMPS:COMPS + 1, :], tile)
+        fix_out[pl.ds(j, COMPS, stride=8), :] = factors * halo_in[slot, 0:COMPS, :]
+        fix_out[pl.ds(4 + j, COMPS, stride=8), :] = 0.25 * factors * near
+    fixes = (fix_out, fix_in, fix_send, fix_recv, 8)
+    pending.extend(exchange(*fixes))
+
+    loads[4].wait()
+    loads[5].wait()
+    high, low = split(jnp.transpose(zonal_raw[...]))
+    zonal_w[0:128, 0:128] = high
+    zonal_w[0:128, 128:256] = low
+    zonal_w[128:256, 0:128] = high
+    zonal_w[128:256, 128:256] = jnp.zeros((LANES, LANES), jnp.bfloat16)
+    for start in range(0, LM, 64):
+        high, low = split(mer_raw[start:start + 64, :])
+        mer_high[start:start + 64, :] = high
+        mer_low[start:start + 64, :] = low
+
+    for peer in peers:
+        await_piece(peer, *fwd)
+    for peer in peers:
+        await_piece(peer, *fixes)
+    for j in range(4):
+        fix[j * RANKS:(j + 1) * RANKS, :] = fix_in[pl.ds(j, RANKS, stride=8), :]
+    for owner in range(RANKS):
+        edge_terms(owner, 0)
+    solve(0)
+    ret = (ret_out.at[0], ret_in.at[0], ret_send.at[0], ret_recv.at[0], ROWS)
+    pending.extend(exchange(*ret))
+
+    for owner in range(RANKS):
+        value = ret_out[0, owner * ROWS:(owner + 1) * ROWS, :]
+        end_out[owner:owner + 1, :] = jnp.sum(
+            columns_to_lanes(value[:, 0:1], 0) + columns_to_lanes(value[:, LANES - 1:LANES], 32), axis=0, keepdims=True
+        )
+    end_out[16:17, :] = ret_out[0, 0:1, :]
+    end_out[17:24, :] = jnp.broadcast_to(ret_out[0, LM - 1:LM, :], (7, LANES))
+    ends = []
+    for slot, device in ((0, east), (1, west), (2, across)):
+        copy = remote(end_out, end_in.at[slot], end_send.at[slot], end_recv.at[slot], device)
+        copy.start()
+        ends.append(copy)
+    pending.extend(ends)
+
+    for peer in peers:
+        await_piece(peer, *ret)
+    for r in range(ROWS):
+        step = ret_in[0, pl.ds(r, COMPS, stride=ROWS), :]
+        set_state(1, r, cur[0, comps(r), :] + 0.25 * spread(wet, r) * step)
+    friction()
+    local_residual(1)
+    fwd = (fwd_out.at[1], fwd_in.at[1], fwd_send.at[1], fwd_recv.at[1], ROWS)
+    pending.extend(exchange(*fwd))
+
+    for copy in ends:
+        copy.wait_recv()
+    norths = jnp.concatenate([end_in[2, 17:18, :], ret_out[0, pl.ds(ROWS - 1, RANKS, stride=ROWS), :][:RANKS - 1]], axis=0)
+    souths = jnp.concatenate([ret_out[0, pl.ds(0, RANKS, stride=ROWS), :][1:], end_in[2, 16:17, :]], axis=0)
+    steps = (shift(end_in[0, 0:RANKS, :], LANES - 32), end_in[1, 0:RANKS, :], norths, souths)
+    for j, step in enumerate(steps):
+        fix[j * RANKS:(j + 1) * RANKS, :] = (
+            fix_in[pl.ds(j, RANKS, stride=8), :] + fix_in[pl.ds(4 + j, RANKS, stride=8), :] * step
+        )
+    edge_terms(rank, 1)
+    for peer in peers[::-1]:
+        await_piece(peer, *fwd)
+        edge_terms(peer, 1)
+    solve(1)
+    ret = (ret_out.at[1], ret_in.at[1], ret_send.at[1], ret_recv.at[1], ROWS)
+    pending.extend(exchange(*ret))
+    for peer in peers:
+        await_piece(peer, *ret)
     for c in range(COMPS):
         rows = pl.ds(c * ROWS, ROWS)
-        state = cur[last, pl.ds(c, ROWS, stride=COMPS), :]
-        out_ref[rows, :] = state + 0.25 * wet[...] * ret_in[last, rows, :]
+        state = cur[1, pl.ds(c, ROWS, stride=COMPS), :]
+        out_ref[rows, :] = state + 0.25 * wet[...] * ret_in[1, rows, :]
     for copy in pending:
         copy.wait_send()
 
@@ -361,16 +437,25 @@
             pltpu.VMEM((LANES, ROWS * LANES), bf16),
             pltpu.VMEM((COMPS, ROWS * LANES), f32),
             pltpu.VMEM(flat, f32),
-            pltpu.VMEM((ITERS, 2, COMPS, LANES), f32),
-            pltpu.VMEM((ITERS, 2, COMPS, LANES), f32),
-            pltpu.VMEM((ITERS, 2, COMPS, LANES), f32),
+            pltpu.VMEM((4, COMPS + 8, LANES), f32),
+            pltpu.VMEM((4, COMPS + 8, LANES), f32),
+            pltpu.VMEM((8 * RANKS, LANES), f32),
+            pltpu.VMEM((8 * RANKS, LANES), f32),
+            pltpu.VMEM((4 * RANKS, LANES), f32),
+            pltpu.VMEM((RANKS + 8, LANES), f32),
+            pltpu.VMEM((3, RANKS + 8, LANES), f32),
+            pltpu.VMEM((LM, 2 * LANES), bf16),
             pltpu.VMEM((ITERS,) + flat, f32),
             pltpu.VMEM((ITERS,) + flat, f32),
             pltpu.VMEM((ITERS,) + flat, f32),
             pltpu.VMEM((ITERS,) + flat, f32),
             dma((6,)),
-            dma((ITERS, 4)),
-            dma((ITERS, 4)),
+            dma((4,)),
+            dma((4,)),
+            dma((RANKS,)),
+            dma((RANKS,)),
+            dma((3,)),
+            dma((3,)),
             dma((ITERS, RANKS)),
             dma((ITERS, RANKS)),
             dma((ITERS, RANKS)),

time: 67.2 us -> 64.4 us (0.958)
  Pallas kernels: 65.3 us -> 62.5 us
    pallas_call x1, Pallas kernels: 65.3 us -> 62.5 us  [body(): pl.pallas_call(kernel, out_shape=jax.ShapeDtypeStruct(flat, f32), in_spec...]
where the time goes in v2:
time: 64.4 us; the launch traced here: 64.2 us
  Pallas kernels  62.5 us (97%)
  local copies, waits for them, and re-layouts  1.67 us (3%)
    pallas_call x1, Pallas kernels, body(): pl.pallas_call(kernel, out_shape=jax.ShapeDtypeStruct(flat, f32), in_spec...  62.5 us
    unnamed x1, local copies, waits for them, and re-layouts  1.67 us

profile of v2, /device:TPU:1, one launch (start us, length us, event | category | flops | bytes accessed | tf_op | source)
XLA Modules:
  0.0 64.2 jit_solution(7326432791092516165)
XLA Ops:
  0.0 62.5 %shard_map.91 = f32[512,128]{1,0:T(8,128)} custom-call(f32[512,128]{1,0:T(8,128)} %bitcast.4, f32[512,128]{1,0:T(8,128)} %bitcast.5, s32[32,128]{1,0:T(8,128)} %wet_hbm.1, s32[32,128]{1,0:T(8,128)} %band_hbm.1, f32[8]{0:T(128)} %drag_ref.1, f32[8]{0:T(128)} %stiff_ref.1, f32[48]{0:T(128)} %times_ref.1, f32[8,128,128]{2,1,0:T(8,128)} %zonal_hbm.1, ...), custom_call_target="tpu_custom_call" | custom-call | flops 600000000 | bytes 2500000 | tf_op jit(solution)/shard_map/pallas_call | solution.py:416
  62.5 1.7 %copy.11 = f32[8,2,32,128]{3,2,1,0:T(8,128)} copy(f32[8,2,32,128]{3,2,1,0:T(8,128)} %bitcast.3) | data formatting | bytes 524288

commit v3 on v2

--- a/solution.py
+++ b/solution.py
@@ -10,6 +10,7 @@
 MESH = pl.DeviceIdType.MESH
 ITERS = 2
 ROWS = 32
+HALF = 16
 LANES = 128
 COMPS = 16
 SAMPLES = 48
@@ -106,9 +107,9 @@
     out_ref,
     tide, forcing, wet_int, band, zonal_raw, mer_raw,
     wet, drag, stiff, ahead, back, zonal_w, mer_high, mer_low,
-    cur, mix, back_terms, terms, halo_out, halo_in, fix_out, fix_in, fix, end_out, end_in, zonal_lhs,
+    cur, mix, back_terms, terms, halo_out, halo_in, fix_out, fix_in, fix, end_out, end_in, mid_out, mid_in, mid, zonal_lhs,
     fwd_out, fwd_in, ret_out, ret_in,
-    local_sem, halo_send, halo_recv, fix_send, fix_recv, end_send, end_recv, fwd_send, fwd_recv, ret_send, ret_recv,
+    local_sem, halo_send, halo_recv, fix_send, fix_recv, end_send, end_recv, mid_send, mid_recv, fwd_send, fwd_recv, ret_send, ret_recv,
 ):
     samp = lax.axis_index("samp")
     space = lax.axis_index("space")
@@ -212,8 +213,35 @@
             {"space": base + peer},
         ).wait_recv()
 
-    def friction():
-        for start in range(0, ROWS, 4):
+    def exchange_half(half, source, target, send, recv, spot):
+        copies = []
+        for peer in peers:
+            copy = remote(
+                source.at[spot(half, peer), :], target.at[place(half, rank), :], send.at[half, peer],
+                recv.at[half, rank], {"space": base + peer},
+            )
+            copy.start()
+            copies.append(copy)
+        target[place(half, rank), :] = source[spot(half, rank), :]
+        return copies
+
+    def await_half(half, peer, source, target, send, recv, spot):
+        remote(
+            source.at[spot(half, rank), :], target.at[place(half, peer), :], send.at[half, peer],
+            recv.at[half, peer], {"space": base + peer},
+        ).wait_recv()
+
+    def place(half, rank_index):
+        return pl.ds(pl.multiple_of(rank_index * ROWS + half * HALF, HALF), HALF)
+
+    def solved(half, rank_index):
+        return pl.ds(pl.multiple_of(half * RANKS * HALF + rank_index * HALF, HALF), HALF)
+
+    def solved_rows(half, owner):
+        return pl.ds(half * RANKS * HALF + owner * HALF, HALF)
+
+    def friction(low_row=0, high_row=ROWS):
+        for start in range(low_row, high_row, 4):
             cols = pl.ds(start * LANES, 4 * LANES)
             both = jnp.dot(ahead[...], mix[0:32, cols], preferred_element_type=jnp.float32)
             velocity = both[:SAMPLES] + both[SAMPLES:]
@@ -227,24 +255,25 @@
             both = jnp.dot(back[...], mix[:, cols], preferred_element_type=jnp.float32)
             back_terms[:, cols] = both[:COMPS] + both[COMPS:]
 
-    def local_residual(it):
-        for r in range(ROWS):
+    def local_terms(it, low_row, high_row):
+        for r in range(low_row, high_row):
             value = cur[it, comps(r), :]
             left = jnp.where(lane == 0, 0.0, shift(value, 1))
             right = jnp.where(lane == LANES - 1, 0.0, shift(value, LANES - 1))
             neighbours = left + right
             if r > 0:
                 neighbours = neighbours + cur[it, comps(r - 1), :]
-            if r < ROWS - 1:
+            if r < high_row - 1:
                 neighbours = neighbours + cur[it, comps(r + 1), :]
             total = value + back_terms[:, pl.ds(r * LANES, LANES)] + spread(stiff, r) * (4.0 * value - neighbours)
             terms[comps(r), :] = total
-        if it == 0:
-            loads[3].wait()
+
+    def local_residual(it, low_row, high_row):
+        count = high_row - low_row
         for c in range(COMPS):
-            rows = pl.ds(c * ROWS, ROWS)
-            fallen = terms[pl.ds(c, ROWS, stride=COMPS), :]
-            fwd_out[it, rows, :] = wet[...] * (forcing[rows, :] - fallen)
+            rows = pl.ds(c * ROWS + low_row, count)
+            fallen = terms[pl.ds(low_row * COMPS + c, count, stride=COMPS), :]
+            fwd_out[it, rows, :] = wet[low_row:high_row] * (forcing[rows, :] - fallen)
 
     def edge_terms(owner, it):
         value = fwd_in[it, piece(owner), :]
@@ -257,6 +286,9 @@
         east_col = jnp.sum(jnp.where(same, east_row, 0.0), axis=1, keepdims=True)
         value = value + jnp.where(block_lane == 0, west_col, 0.0) + jnp.where(block_lane == LANES - 1, east_col, 0.0)
         value = value + jnp.where(block_row == 0, north_row, 0.0) + jnp.where(block_row == ROWS - 1, south_row, 0.0)
+        if it == 1:
+            mid_row = jnp.broadcast_to(mid[pl.ds(owner, 1), :], block)
+            value = value + jnp.where(block_row == HALF - 1, mid_row, 0.0)
         high, low = split(value)
         zonal_lhs[piece(owner), 0:LANES] = high
         zonal_lhs[piece(owner), LANES:2 * LANES] = low
@@ -264,9 +296,18 @@
     def solve(it):
         both = jnp.dot(zonal_lhs[...], zonal_w[...], preferred_element_type=jnp.float32)
         high, low = split(both[:, :LANES] + both[:, LANES:])
-        both = jnp.dot(mer_high[...], jnp.concatenate([high, low], axis=1), preferred_element_type=jnp.float32)
-        third = jnp.dot(mer_low[...], high, preferred_element_type=jnp.float32)
-        ret_out[it] = both[:, :LANES] + both[:, LANES:] + third
+        pair = jnp.concatenate([high, low], axis=1)
+        copies = []
+        for half in range(2):
+            rows = pl.ds(half * RANKS * HALF, RANKS * HALF)
+            both = jnp.dot(mer_high[rows, :], pair, preferred_element_type=jnp.float32)
+            third = jnp.dot(mer_low[rows, :], high, preferred_element_type=jnp.float32)
+            ret_out[it, rows, :] = both[:, :LANES] + both[:, LANES:] + third
+            copies.extend(exchange_half(half, *returns(it)))
+        return copies
+
+    def returns(it):
+        return ret_out.at[it], ret_in.at[it], ret_send.at[it], ret_recv.at[it], solved
 
     pending = []
     loads[2].wait()
@@ -303,8 +344,10 @@
         copy.start()
         halos.append(copy)
     pending.extend(halos)
-    local_residual(0)
-    fwd = (fwd_out.at[0], fwd_in.at[0], fwd_send.at[0], fwd_recv.at[0], ROWS)
+    local_terms(0, 0, ROWS)
+    loads[3].wait()
+    local_residual(0, 0, ROWS)
+    fwd = (fwd_out.at[0], fwd_in.at[0], fwd_send.at[0, 0], fwd_recv.at[0, 0], ROWS)
     pending.extend(exchange(*fwd))
 
     for copy in halos:
@@ -322,6 +365,13 @@
         fix_out[pl.ds(4 + j, COMPS, stride=8), :] = 0.25 * factors * near
     fixes = (fix_out, fix_in, fix_send, fix_recv, 8)
     pending.extend(exchange(*fixes))
+    factors = jnp.broadcast_to(strength[HALF - 1:HALF], tile)
+    mid_out[pl.ds(0, COMPS, stride=8), :] = factors * cur[0, comps(HALF), :]
+    mid_out[pl.ds(1, COMPS, stride=8), :] = 0.25 * factors * jnp.broadcast_to(wets[HALF:HALF + 1], tile)
+    for j in range(2, 8):
+        mid_out[pl.ds(j, COMPS, stride=8), :] = jnp.zeros(tile, jnp.float32)
+    mids = (mid_out, mid_in, mid_send, mid_recv, 8)
+    pending.extend(exchange(*mids))
 
     loads[4].wait()
     loads[5].wait()
@@ -330,10 +380,12 @@
     zonal_w[0:128, 128:256] = low
     zonal_w[128:256, 0:128] = high
     zonal_w[128:256, 128:256] = jnp.zeros((LANES, LANES), jnp.bfloat16)
-    for start in range(0, LM, 64):
-        high, low = split(mer_raw[start:start + 64, :])
-        mer_high[start:start + 64, :] = high
-        mer_low[start:start + 64, :] = low
+    for owner in range(RANKS):
+        for half in range(2):
+            start = owner * ROWS + half * HALF
+            high, low = split(mer_raw[start:start + HALF, :])
+            mer_high[solved_rows(half, owner), :] = high
+            mer_low[solved_rows(half, owner), :] = low
 
     for peer in peers:
         await_piece(peer, *fwd)
@@ -343,12 +395,10 @@
         fix[j * RANKS:(j + 1) * RANKS, :] = fix_in[pl.ds(j, RANKS, stride=8), :]
     for owner in range(RANKS):
         edge_terms(owner, 0)
-    solve(0)
-    ret = (ret_out.at[0], ret_in.at[0], ret_send.at[0], ret_recv.at[0], ROWS)
-    pending.extend(exchange(*ret))
+    pending.extend(solve(0))
 
     for owner in range(RANKS):
-        value = ret_out[0, owner * ROWS:(owner + 1) * ROWS, :]
+        value = jnp.concatenate([ret_out[0, solved_rows(0, owner), :], ret_out[0, solved_rows(1, owner), :]], axis=0)
         end_out[owner:owner + 1, :] = jnp.sum(
             columns_to_lanes(value[:, 0:1], 0) + columns_to_lanes(value[:, LANES - 1:LANES], 32), axis=0, keepdims=True
         )
@@ -361,38 +411,45 @@
         ends.append(copy)
     pending.extend(ends)
 
+    for half in range(2):
+        for peer in peers:
+            await_half(half, peer, *returns(0))
+        low_row, high_row = half * HALF, (half + 1) * HALF
+        for r in range(low_row, high_row):
+            step = ret_in[0, pl.ds(r, COMPS, stride=ROWS), :]
+            set_state(1, r, cur[0, comps(r), :] + 0.25 * spread(wet, r) * step)
+        friction(low_row, high_row)
+        local_terms(1, low_row, high_row)
+        local_residual(1, low_row, high_row)
+        pending.extend(exchange_half(half, fwd_out.at[1], fwd_in.at[1], fwd_send.at[1], fwd_recv.at[1], place))
+
     for peer in peers:
-        await_piece(peer, *ret)
-    for r in range(ROWS):
-        step = ret_in[0, pl.ds(r, COMPS, stride=ROWS), :]
-        set_state(1, r, cur[0, comps(r), :] + 0.25 * spread(wet, r) * step)
-    friction()
-    local_residual(1)
-    fwd = (fwd_out.at[1], fwd_in.at[1], fwd_send.at[1], fwd_recv.at[1], ROWS)
-    pending.extend(exchange(*fwd))
-
+        await_piece(peer, *mids)
     for copy in ends:
         copy.wait_recv()
-    norths = jnp.concatenate([end_in[2, 17:18, :], ret_out[0, pl.ds(ROWS - 1, RANKS, stride=ROWS), :][:RANKS - 1]], axis=0)
-    souths = jnp.concatenate([ret_out[0, pl.ds(0, RANKS, stride=ROWS), :][1:], end_in[2, 16:17, :]], axis=0)
+    norths = jnp.concatenate([end_in[2, 17:18, :], ret_out[0, pl.ds(RANKS * HALF + HALF - 1, RANKS, stride=HALF), :][:RANKS - 1]], axis=0)
+    souths = jnp.concatenate([ret_out[0, pl.ds(0, RANKS, stride=HALF), :][1:], end_in[2, 16:17, :]], axis=0)
     steps = (shift(end_in[0, 0:RANKS, :], LANES - 32), end_in[1, 0:RANKS, :], norths, souths)
     for j, step in enumerate(steps):
         fix[j * RANKS:(j + 1) * RANKS, :] = (
             fix_in[pl.ds(j, RANKS, stride=8), :] + fix_in[pl.ds(4 + j, RANKS, stride=8), :] * step
         )
+    mid[...] = mid_in[pl.ds(0, RANKS, stride=8), :] + mid_in[pl.ds(1, RANKS, stride=8), :] * ret_out[
+        0, pl.ds(RANKS * HALF, RANKS, stride=HALF), :
+    ]
     edge_terms(rank, 1)
     for peer in peers[::-1]:
-        await_piece(peer, *fwd)
+        for half in range(2):
+            await_half(half, peer, fwd_out.at[1], fwd_in.at[1], fwd_send.at[1], fwd_recv.at[1], place)
         edge_terms(peer, 1)
-    solve(1)
-    ret = (ret_out.at[1], ret_in.at[1], ret_send.at[1], ret_recv.at[1], ROWS)
-    pending.extend(exchange(*ret))
-    for peer in peers:
-        await_piece(peer, *ret)
-    for c in range(COMPS):
-        rows = pl.ds(c * ROWS, ROWS)
-        state = cur[1, pl.ds(c, ROWS, stride=COMPS), :]
-        out_ref[rows, :] = state + 0.25 * wet[...] * ret_in[1, rows, :]
+    pending.extend(solve(1))
+    for half in range(2):
+        for peer in peers:
+            await_half(half, peer, *returns(1))
+        for c in range(COMPS):
+            rows = pl.ds(c * ROWS + half * HALF, HALF)
+            state = cur[1, pl.ds(half * HALF * COMPS + c, HALF, stride=COMPS), :]
+            out_ref[rows, :] = state + 0.25 * wet[half * HALF:(half + 1) * HALF] * ret_in[1, rows, :]
     for copy in pending:
         copy.wait_send()
 
@@ -415,7 +472,7 @@
     smem = pl.BlockSpec(memory_space=pltpu.SMEM)
     result = pl.pallas_call(
         kernel,
-        out_shape=jax.ShapeDtypeStruct(flat, f32),
+        out_shape=pltpu.VMEM(flat, f32),
         in_specs=[any_spec] * 4 + [smem] * 3 + [any_spec] * 2,
         out_specs=pl.BlockSpec(memory_space=pltpu.VMEM),
         scratch_shapes=[
@@ -444,6 +501,9 @@
             pltpu.VMEM((4 * RANKS, LANES), f32),
             pltpu.VMEM((RANKS + 8, LANES), f32),
             pltpu.VMEM((3, RANKS + 8, LANES), f32),
+            pltpu.VMEM((8 * RANKS, LANES), f32),
+            pltpu.VMEM((8 * RANKS, LANES), f32),
+            pltpu.VMEM((RANKS, LANES), f32),
             pltpu.VMEM((LM, 2 * LANES), bf16),
             pltpu.VMEM((ITERS,) + flat, f32),
             pltpu.VMEM((ITERS,) + flat, f32),
@@ -456,13 +516,15 @@
             dma((RANKS,)),
             dma((3,)),
             dma((3,)),
-            dma((ITERS, RANKS)),
-            dma((ITERS, RANKS)),
-            dma((ITERS, RANKS)),
-            dma((ITERS, RANKS)),
+            dma((RANKS,)),
+            dma((RANKS,)),
+            dma((ITERS, 2, RANKS)),
+            dma((ITERS, 2, RANKS)),
+            dma((ITERS, 2, RANKS)),
+            dma((ITERS, 2, RANKS)),
         ],
         compiler_params=pltpu.CompilerParams(
-            collective_id=0, has_side_effects=True, vmem_limit_bytes=64 * 1024 * 1024
+            collective_id=0, has_side_effects=True, vmem_limit_bytes=60 * 1024 * 1024
         ),
         cost_estimate=pl.CostEstimate(flops=600000000, bytes_accessed=2500000, transcendentals=0),
     )(

time: 64.4 us -> 61.9 us (0.961)
  Pallas kernels: 62.5 us -> 61 us
  local copies, waits for them, and re-layouts: 1.67 us -> 0.71 us
    pallas_call x1, Pallas kernels: 62.5 us -> 61 us  [body(): pl.pallas_call(kernel, out_shape=pltpu.VMEM(flat, f32), in_specs=[any_spe...]
    unnamed x1, local copies, waits for them, and re-layouts: 1.67 us -> 0.71 us
where the time goes in v3:
time: 61.9 us; the launch traced here: 61.7 us
  Pallas kernels  61 us (99%)
  local copies, waits for them, and re-layouts  0.71 us (1%)
    pallas_call x1, Pallas kernels, body(): pl.pallas_call(kernel, out_shape=pltpu.VMEM(flat, f32), in_specs=[any_spe...  61 us

profile of v3, /device:TPU:1, one launch (start us, length us, event | category | flops | bytes accessed | tf_op | source)
XLA Modules:
  0.0 61.7 jit_solution(18346963838484298961)
XLA Ops:
  0.0 61.0 %shard_map.91 = f32[512,128]{1,0:T(8,128)S(1)} custom-call(f32[512,128]{1,0:T(8,128)} %bitcast.4, f32[512,128]{1,0:T(8,128)} %bitcast.5, s32[32,128]{1,0:T(8,128)} %wet_hbm.1, s32[32,128]{1,0:T(8,128)} %band_hbm.1, f32[8]{0:T(128)} %drag_ref.1, f32[8]{0:T(128)} %stiff_ref.1, f32[48]{0:T(128)} %times_ref.1, f32[8,128,128]{2,1,0:T(8,128)} %zonal_hbm.1, ...), custom_call_target="tpu_custom_call" | custom-call | flops 600000000 | bytes 2500000 | tf_op jit(solution)/shard_map/pallas_call | solution.py:473
  61.0 0.7 %copy.11 = f32[8,2,32,128]{3,2,1,0:T(8,128)} copy(f32[8,2,32,128]{3,2,1,0:T(8,128)S(1)} %bitcast.3) | data formatting | bytes 524288

commit v4 on v3

--- a/solution.py
+++ b/solution.py
@@ -107,9 +107,9 @@
     out_ref,
     tide, forcing, wet_int, band, zonal_raw, mer_raw,
     wet, drag, stiff, ahead, back, zonal_w, mer_high, mer_low,
-    cur, mix, back_terms, terms, halo_out, halo_in, fix_out, fix_in, fix, end_out, end_in, mid_out, mid_in, mid, zonal_lhs,
+    cur, mix, back_terms, terms, halo_out, halo_in, fix_out, fix_in, fix, end_out, end_in, rim_out, rim_in, far, late_out, late_in, full, shape_w, shape_e, mid, zonal_lhs,
     fwd_out, fwd_in, ret_out, ret_in,
-    local_sem, halo_send, halo_recv, fix_send, fix_recv, end_send, end_recv, mid_send, mid_recv, fwd_send, fwd_recv, ret_send, ret_recv,
+    local_sem, halo_send, halo_recv, fix_send, fix_recv, end_send, end_recv, rim_send, rim_recv, late_send, late_recv, fwd_send, fwd_recv, ret_send, ret_recv,
 ):
     samp = lax.axis_index("samp")
     space = lax.axis_index("space")
@@ -125,7 +125,7 @@
         pltpu.make_async_copy(band_hbm, band, local_sem.at[1]),
         pltpu.make_async_copy(tide_hbm, tide, local_sem.at[2]),
         pltpu.make_async_copy(forcing_hbm, forcing, local_sem.at[3]),
-        pltpu.make_async_copy(zonal_hbm.at[owned], zonal_raw, local_sem.at[4]),
+        pltpu.make_async_copy(zonal_hbm, zonal_raw, local_sem.at[4]),
         pltpu.make_async_copy(meridional_hbm.at[owned], mer_raw, local_sem.at[5]),
     ]
     for load in loads:
@@ -275,23 +275,34 @@
             fallen = terms[pl.ds(low_row * COMPS + c, count, stride=COMPS), :]
             fwd_out[it, rows, :] = wet[low_row:high_row] * (forcing[rows, :] - fallen)
 
+    def lane_column(row):
+        return jnp.sum(jnp.where(block_lane == block_row, jnp.broadcast_to(row, block), 0.0), axis=1, keepdims=True)
+
     def edge_terms(owner, it):
         value = fwd_in[it, piece(owner), :]
-        west_row = jnp.broadcast_to(fix[pl.ds(owner, 1), :], block)
-        east_row = jnp.broadcast_to(fix[pl.ds(owner + RANKS, 1), :], block)
         north_row = jnp.broadcast_to(fix[pl.ds(owner + 2 * RANKS, 1), :], block)
         south_row = jnp.broadcast_to(fix[pl.ds(owner + 3 * RANKS, 1), :], block)
-        same = block_lane == block_row
-        west_col = jnp.sum(jnp.where(same, west_row, 0.0), axis=1, keepdims=True)
-        east_col = jnp.sum(jnp.where(same, east_row, 0.0), axis=1, keepdims=True)
-        value = value + jnp.where(block_lane == 0, west_col, 0.0) + jnp.where(block_lane == LANES - 1, east_col, 0.0)
         value = value + jnp.where(block_row == 0, north_row, 0.0) + jnp.where(block_row == ROWS - 1, south_row, 0.0)
         if it == 1:
+            west_col = lane_column(fix[pl.ds(owner, 1), :])
+            east_col = lane_column(fix[pl.ds(owner + RANKS, 1), :])
+            value = value + jnp.where(block_lane == 0, west_col, 0.0)
+            value = value + jnp.where(block_lane == LANES - 1, east_col, 0.0)
             mid_row = jnp.broadcast_to(mid[pl.ds(owner, 1), :], block)
             value = value + jnp.where(block_row == HALF - 1, mid_row, 0.0)
         high, low = split(value)
         zonal_lhs[piece(owner), 0:LANES] = high
         zonal_lhs[piece(owner), LANES:2 * LANES] = low
+
+    def meridional(rows, high, pair):
+        both = jnp.dot(mer_high[rows, :], pair, preferred_element_type=jnp.float32)
+        third = jnp.dot(mer_low[rows, :], high, preferred_element_type=jnp.float32)
+        return both[:, :LANES] + both[:, LANES:] + third
+
+    def device_rows(value, owner):
+        first_half = value[owner * HALF:(owner + 1) * HALF]
+        second_half = value[(RANKS + owner) * HALF:(RANKS + owner + 1) * HALF]
+        return jnp.concatenate([first_half, second_half], axis=0)
 
     def solve(it):
         both = jnp.dot(zonal_lhs[...], zonal_w[...], preferred_element_type=jnp.float32)
@@ -300,9 +311,7 @@
         copies = []
         for half in range(2):
             rows = pl.ds(half * RANKS * HALF, RANKS * HALF)
-            both = jnp.dot(mer_high[rows, :], pair, preferred_element_type=jnp.float32)
-            third = jnp.dot(mer_low[rows, :], high, preferred_element_type=jnp.float32)
-            ret_out[it, rows, :] = both[:, :LANES] + both[:, LANES:] + third
+            ret_out[it, rows, :] = meridional(rows, high, pair)
             copies.extend(exchange_half(half, *returns(it)))
         return copies
 
@@ -350,32 +359,60 @@
     fwd = (fwd_out.at[0], fwd_in.at[0], fwd_send.at[0, 0], fwd_recv.at[0, 0], ROWS)
     pending.extend(exchange(*fwd))
 
-    for copy in halos:
-        copy.wait_recv()
-    sides = (
-        (2, shift(packed, 64)),
-        (3, shift(packed, 32)),
-        (0, strength[0:1] * has_north),
-        (1, strength[ROWS - 1:ROWS] * has_south),
-    )
-    for j, (slot, factor) in enumerate(sides):
-        factors = jnp.broadcast_to(factor, tile)
-        near = jnp.broadcast_to(halo_in[slot, COMPS:COMPS + 1, :], tile)
-        fix_out[pl.ds(j, COMPS, stride=8), :] = factors * halo_in[slot, 0:COMPS, :]
-        fix_out[pl.ds(4 + j, COMPS, stride=8), :] = 0.25 * factors * near
+    halo_of = {2: halos[0], 3: halos[1], 0: halos[2], 1: halos[3]}
+    edges = ((0, strength[0:1], rank == 0), (1, strength[ROWS - 1:ROWS], rank == RANKS - 1))
+
+    def edge_row(slot, factor):
+        return jnp.broadcast_to(factor, tile) * halo_in[slot, 0:COMPS, :]
+
+    def edge_factor(slot, factor):
+        return 0.25 * jnp.broadcast_to(factor * halo_in[slot, COMPS:COMPS + 1, :], tile)
+
+    for slot, factor, is_far in edges:
+        @pl.when(is_far)
+        def _():
+            rim_out[pl.ds(slot, COMPS, stride=8), :] = jnp.zeros(tile, jnp.float32)
+
+        @pl.when(jnp.logical_not(is_far))
+        def _():
+            halo_of[slot].wait_recv()
+            rim_out[pl.ds(slot, COMPS, stride=8), :] = edge_row(slot, factor)
+
+    factors = jnp.broadcast_to(strength[HALF - 1:HALF], tile)
+    rim_out[pl.ds(2, COMPS, stride=8), :] = factors * cur[0, comps(HALF), :]
+    rim_out[pl.ds(3, COMPS, stride=8), :] = 0.25 * factors * jnp.broadcast_to(wets[HALF:HALF + 1], tile)
+    for j in range(4, 8):
+        rim_out[pl.ds(j, COMPS, stride=8), :] = jnp.zeros(tile, jnp.float32)
+    rims = (rim_out, rim_in, rim_send, rim_recv, 8)
+    pending.extend(exchange(*rims))
+
+    far[...] = jnp.zeros(tile, jnp.float32)
+    for slot, factor, is_far in edges:
+        @pl.when(is_far)
+        def _():
+            halo_of[slot].wait_recv()
+            far[...] = edge_row(slot, factor * (has_north if slot == 0 else has_south))
+
+    halo_of[2].wait_recv()
+    halo_of[3].wait_recv()
+    west_factor, east_factor = shift(packed, 64), shift(packed, 32)
+    for j, value in enumerate((
+        edge_row(2, west_factor),
+        edge_row(3, east_factor),
+        far[...],
+        edge_factor(2, west_factor),
+        edge_factor(3, east_factor),
+        edge_factor(0, strength[0:1] * has_north),
+        edge_factor(1, strength[ROWS - 1:ROWS] * has_south),
+        jnp.zeros(tile, jnp.float32),
+    )):
+        fix_out[pl.ds(j, COMPS, stride=8), :] = value
     fixes = (fix_out, fix_in, fix_send, fix_recv, 8)
     pending.extend(exchange(*fixes))
-    factors = jnp.broadcast_to(strength[HALF - 1:HALF], tile)
-    mid_out[pl.ds(0, COMPS, stride=8), :] = factors * cur[0, comps(HALF), :]
-    mid_out[pl.ds(1, COMPS, stride=8), :] = 0.25 * factors * jnp.broadcast_to(wets[HALF:HALF + 1], tile)
-    for j in range(2, 8):
-        mid_out[pl.ds(j, COMPS, stride=8), :] = jnp.zeros(tile, jnp.float32)
-    mids = (mid_out, mid_in, mid_send, mid_recv, 8)
-    pending.extend(exchange(*mids))
 
     loads[4].wait()
     loads[5].wait()
-    high, low = split(jnp.transpose(zonal_raw[...]))
+    high, low = split(jnp.transpose(zonal_raw[owned]))
     zonal_w[0:128, 0:128] = high
     zonal_w[0:128, 128:256] = low
     zonal_w[128:256, 0:128] = high
@@ -387,23 +424,73 @@
             mer_high[solved_rows(half, owner), :] = high
             mer_low[solved_rows(half, owner), :] = low
 
+    square = (LANES, LANES)
+    diagonal = iota(square, 0) == iota(square, 1)
+    for k in range(COMPS // 2):
+        for column, shape_ref in ((0, shape_w), (LANES - 1, shape_e)):
+            values = jnp.broadcast_to(zonal_raw[k][:, column:column + 1], square)
+            row = jnp.sum(jnp.where(diagonal, values, 0.0), axis=0, keepdims=True)
+            shape_ref[2 * k:2 * k + 2, :] = jnp.broadcast_to(row, (2, LANES))
+
     for peer in peers:
         await_piece(peer, *fwd)
     for peer in peers:
-        await_piece(peer, *fixes)
-    for j in range(4):
-        fix[j * RANKS:(j + 1) * RANKS, :] = fix_in[pl.ds(j, RANKS, stride=8), :]
+        await_piece(peer, *rims)
+    for j in range(2):
+        fix[(2 + j) * RANKS:(3 + j) * RANKS, :] = rim_in[pl.ds(j, RANKS, stride=8), :]
     for owner in range(RANKS):
         edge_terms(owner, 0)
     pending.extend(solve(0))
 
+    for peer in peers:
+        await_piece(peer, *fixes)
+    lower = (space >= RANKS).astype(jnp.float32)
+    upper = 1.0 - lower
     for owner in range(RANKS):
-        value = jnp.concatenate([ret_out[0, solved_rows(0, owner), :], ret_out[0, solved_rows(1, owner), :]], axis=0)
+        west_col = lane_column(fix_in[owner * 8:owner * 8 + 1, :])
+        east_col = lane_column(fix_in[owner * 8 + 1:owner * 8 + 2, :])
+        value = jnp.where(block_lane == 0, west_col, 0.0) + jnp.where(block_lane == 1, east_col, 0.0)
+        if owner == 0:
+            value = value + jnp.where((block_lane == 2) & (block_row == 0), lower, 0.0)
+        if owner == RANKS - 1:
+            value = value + jnp.where((block_lane == 2) & (block_row == ROWS - 1), upper, 0.0)
+        high, low = split(value)
+        zonal_lhs[piece(owner), 0:LANES] = high
+        zonal_lhs[piece(owner), LANES:2 * LANES] = low
+    heights = meridional(pl.ds(0, LM), zonal_lhs[:, 0:LANES], zonal_lhs[...])
+    crossing = fix_in[2:3, :] + fix_in[(RANKS - 1) * 8 + 2:(RANKS - 1) * 8 + 3, :]
+    high, low = split(jnp.broadcast_to(crossing, tile))
+    both = jnp.dot(jnp.concatenate([high, low], axis=1), zonal_w[...], preferred_element_type=jnp.float32)
+    crossing = (both[:, :LANES] + both[:, LANES:])[0:1]
+    for owner in range(RANKS):
+        value = device_rows(heights, owner)
+        along = jnp.sum(
+            columns_to_lanes(value[:, 0:1], 0)
+            + columns_to_lanes(value[:, 1:2], 32)
+            + columns_to_lanes(value[:, 2:3], 64),
+            axis=0,
+            keepdims=True,
+        )
+        late_out[owner * 8:owner * 8 + 1, :] = along
+        late_out[owner * 8 + 1:owner * 8 + 8, :] = jnp.broadcast_to(crossing, (7, LANES))
+    lates = (late_out, late_in, late_send, late_recv, 8)
+    pending.extend(exchange(*lates))
+
+    mine = pl.ds(rank, 1)
+    flat = (LM, LANES)
+    full[...] = (
+        ret_out[0]
+        + jnp.broadcast_to(heights[:, 0:1], flat) * jnp.broadcast_to(shape_w[mine, :], flat)
+        + jnp.broadcast_to(heights[:, 1:2], flat) * jnp.broadcast_to(shape_e[mine, :], flat)
+        + jnp.broadcast_to(heights[:, 2:3], flat) * jnp.broadcast_to(crossing, flat)
+    )
+    for owner in range(RANKS):
+        value = jnp.concatenate([full[solved_rows(0, owner), :], full[solved_rows(1, owner), :]], axis=0)
         end_out[owner:owner + 1, :] = jnp.sum(
             columns_to_lanes(value[:, 0:1], 0) + columns_to_lanes(value[:, LANES - 1:LANES], 32), axis=0, keepdims=True
         )
-    end_out[16:17, :] = ret_out[0, 0:1, :]
-    end_out[17:24, :] = jnp.broadcast_to(ret_out[0, LM - 1:LM, :], (7, LANES))
+    end_out[16:17, :] = full[0:1, :]
+    end_out[17:24, :] = jnp.broadcast_to(full[LM - 1:LM, :], (7, LANES))
     ends = []
     for slot, device in ((0, east), (1, west), (2, across)):
         copy = remote(end_out, end_in.at[slot], end_send.at[slot], end_recv.at[slot], device)
@@ -414,28 +501,40 @@
     for half in range(2):
         for peer in peers:
             await_half(half, peer, *returns(0))
+        if half == 0:
+            for peer in peers:
+                await_piece(peer, *lates)
+            along = late_in[pl.ds(0, COMPS, stride=8), :]
+            shapes = (shape_w[...], shape_e[...], late_in[pl.ds(1, COMPS, stride=8), :])
         low_row, high_row = half * HALF, (half + 1) * HALF
         for r in range(low_row, high_row):
             step = ret_in[0, pl.ds(r, COMPS, stride=ROWS), :]
+            for j, shape in enumerate(shapes):
+                step = step + jnp.broadcast_to(along[:, ROWS * j + r:ROWS * j + r + 1], tile) * shape
             set_state(1, r, cur[0, comps(r), :] + 0.25 * spread(wet, r) * step)
         friction(low_row, high_row)
         local_terms(1, low_row, high_row)
         local_residual(1, low_row, high_row)
         pending.extend(exchange_half(half, fwd_out.at[1], fwd_in.at[1], fwd_send.at[1], fwd_recv.at[1], place))
 
-    for peer in peers:
-        await_piece(peer, *mids)
     for copy in ends:
         copy.wait_recv()
-    norths = jnp.concatenate([end_in[2, 17:18, :], ret_out[0, pl.ds(RANKS * HALF + HALF - 1, RANKS, stride=HALF), :][:RANKS - 1]], axis=0)
-    souths = jnp.concatenate([ret_out[0, pl.ds(0, RANKS, stride=HALF), :][1:], end_in[2, 16:17, :]], axis=0)
+    norths = jnp.concatenate(
+        [end_in[2, 17:18, :], full[pl.ds(RANKS * HALF + HALF - 1, RANKS, stride=HALF), :][:RANKS - 1]], axis=0
+    )
+    souths = jnp.concatenate([full[pl.ds(0, RANKS, stride=HALF), :][1:], end_in[2, 16:17, :]], axis=0)
+    crossed = fix_in[pl.ds(2, RANKS, stride=8), :]
+    bases = (
+        fix_in[pl.ds(0, RANKS, stride=8), :],
+        fix_in[pl.ds(1, RANKS, stride=8), :],
+        rim_in[pl.ds(0, RANKS, stride=8), :] + lower * crossed,
+        rim_in[pl.ds(1, RANKS, stride=8), :] + upper * crossed,
+    )
     steps = (shift(end_in[0, 0:RANKS, :], LANES - 32), end_in[1, 0:RANKS, :], norths, souths)
-    for j, step in enumerate(steps):
-        fix[j * RANKS:(j + 1) * RANKS, :] = (
-            fix_in[pl.ds(j, RANKS, stride=8), :] + fix_in[pl.ds(4 + j, RANKS, stride=8), :] * step
-        )
-    mid[...] = mid_in[pl.ds(0, RANKS, stride=8), :] + mid_in[pl.ds(1, RANKS, stride=8), :] * ret_out[
-        0, pl.ds(RANKS * HALF, RANKS, stride=HALF), :
+    for j in range(4):
+        fix[j * RANKS:(j + 1) * RANKS, :] = bases[j] + fix_in[pl.ds(3 + j, RANKS, stride=8), :] * steps[j]
+    mid[...] = rim_in[pl.ds(2, RANKS, stride=8), :] + rim_in[pl.ds(3, RANKS, stride=8), :] * full[
+        pl.ds(RANKS * HALF, RANKS, stride=HALF), :
     ]
     edge_terms(rank, 1)
     for peer in peers[::-1]:
@@ -480,7 +579,7 @@
             pltpu.VMEM(flat, f32),
             pltpu.VMEM((ROWS, LANES), jnp.int32),
             pltpu.VMEM((ROWS, LANES), jnp.int32),
-            pltpu.VMEM((LANES, LANES), f32),
+            pltpu.VMEM((COMPS // 2, LANES, LANES), f32),
             pltpu.VMEM((LM, LM), f32),
             pltpu.VMEM((ROWS, LANES), f32),
             pltpu.VMEM((ROWS, LANES), f32),
@@ -503,6 +602,12 @@
             pltpu.VMEM((3, RANKS + 8, LANES), f32),
             pltpu.VMEM((8 * RANKS, LANES), f32),
             pltpu.VMEM((8 * RANKS, LANES), f32),
+            pltpu.VMEM((COMPS, LANES), f32),
+            pltpu.VMEM((8 * RANKS, LANES), f32),
+            pltpu.VMEM((8 * RANKS, LANES), f32),
+            pltpu.VMEM(flat, f32),
+            pltpu.VMEM((COMPS, LANES), f32),
+            pltpu.VMEM((COMPS, LANES), f32),
             pltpu.VMEM((RANKS, LANES), f32),
             pltpu.VMEM((LM, 2 * LANES), bf16),
             pltpu.VMEM((ITERS,) + flat, f32),
@@ -516,6 +621,8 @@
             dma((RANKS,)),
             dma((3,)),
             dma((3,)),
+            dma((RANKS,)),
+            dma((RANKS,)),
             dma((RANKS,)),
             dma((RANKS,)),
             dma((ITERS, 2, RANKS)),

time: 61.9 us -> 63.1 us (1.019)
  Pallas kernels: 61 us -> 62.2 us
    pallas_call x1, Pallas kernels: 61 us -> 62.2 us  [body(): pl.pallas_call(kernel, out_shape=pltpu.VMEM(flat, f32), in_specs=[any_spe...]
where the time goes in v4:
time: 63.1 us; the launch traced here: 63 us
  Pallas kernels  62.2 us (99%)
  local copies, waits for them, and re-layouts  0.71 us (1%)
    pallas_call x1, Pallas kernels, body(): pl.pallas_call(kernel, out_shape=pltpu.VMEM(flat, f32), in_specs=[any_spe...  62.2 us

profile of v4, /device:TPU:1, one launch (start us, length us, event | category | flops | bytes accessed | tf_op | source)
XLA Modules:
  0.0 63.0 jit_solution(4738448776356320582)
XLA Ops:
  0.0 62.2 %shard_map.91 = f32[512,128]{1,0:T(8,128)S(1)} custom-call(f32[512,128]{1,0:T(8,128)} %bitcast.4, f32[512,128]{1,0:T(8,128)} %bitcast.5, s32[32,128]{1,0:T(8,128)} %wet_hbm.1, s32[32,128]{1,0:T(8,128)} %band_hbm.1, f32[8]{0:T(128)} %drag_ref.1, f32[8]{0:T(128)} %stiff_ref.1, f32[48]{0:T(128)} %times_ref.1, f32[8,128,128]{2,1,0:T(8,128)} %zonal_hbm.1, ...), custom_call_target="tpu_custom_call" | custom-call | flops 600000000 | bytes 2500000 | tf_op jit(solution)/shard_map/pallas_call | solution.py:572
  62.3 0.7 %copy.11 = f32[8,2,32,128]{3,2,1,0:T(8,128)} copy(f32[8,2,32,128]{3,2,1,0:T(8,128)S(1)} %bitcast.3) | data formatting | bytes 524288

commit v5 on v3

--- a/solution.py
+++ b/solution.py
@@ -145,20 +145,8 @@
     for target in [north, south, west, east, across] + [{"space": base + peer} for peer in peers]:
         pl.semaphore_signal(barrier, inc=1, device_id=target, device_id_type=MESH)
 
-    build_factors(times_ref, ahead, back)
-
     loads[0].wait()
-    loads[1].wait()
     wet[...] = wet_int[...].astype(jnp.float32)
-    drags = jnp.zeros((ROWS, LANES), jnp.float32)
-    stiffs = jnp.zeros((ROWS, LANES), jnp.float32)
-    for level in range(drag_ref.shape[0]):
-        here = band[...] == level
-        drags = jnp.where(here, drag_ref[level], drags)
-        stiffs = jnp.where(here, stiff_ref[level], stiffs)
-    drag[...] = drags * (2.0 / SAMPLES)
-    stiff[...] = stiffs
-
     tile = (COMPS, LANES)
     lane = iota(tile, 1)
     block = (ROWS, LANES)
@@ -319,24 +307,17 @@
         first = jnp.where(lane == r, shift(value, r), first)
         last = jnp.where(lane == r, shift(value, r + 1), last)
     wets = wet[...]
-    strength = wets * stiff[...]
-    packed = jnp.sum(
-        columns_to_lanes(wets[:, 0:1], 0)
-        + columns_to_lanes(wets[:, LANES - 1:LANES], 32)
-        + columns_to_lanes(strength[:, 0:1], 64)
-        + columns_to_lanes(strength[:, LANES - 1:LANES], 96),
-        axis=0,
-        keepdims=True,
+    near_wets = jnp.sum(
+        columns_to_lanes(wets[:, 0:1], 0) + columns_to_lanes(wets[:, LANES - 1:LANES], 32), axis=0, keepdims=True
     )
     for slot, value, extra in (
         (0, cur[0, comps(ROWS - 1), :], wets[ROWS - 1:ROWS]),
         (1, cur[0, comps(0), :], wets[0:1]),
-        (2, last, shift(packed, LANES - 32)),
-        (3, first, packed),
+        (2, last, shift(near_wets, LANES - 32)),
+        (3, first, near_wets),
     ):
         halo_out[slot, 0:COMPS, :] = value
         halo_out[slot, COMPS:COMPS + 8, :] = jnp.broadcast_to(extra, (8, LANES))
-    friction()
     pl.semaphore_wait(barrier, 5 + len(peers))
     halos = []
     for slot, device in ((2, east), (3, west), (0, south), (1, north)):
@@ -344,6 +325,21 @@
         copy.start()
         halos.append(copy)
     pending.extend(halos)
+    build_factors(times_ref, ahead, back)
+    loads[1].wait()
+    drags = jnp.zeros((ROWS, LANES), jnp.float32)
+    stiffs = jnp.zeros((ROWS, LANES), jnp.float32)
+    for level in range(drag_ref.shape[0]):
+        here = band[...] == level
+        drags = jnp.where(here, drag_ref[level], drags)
+        stiffs = jnp.where(here, stiff_ref[level], stiffs)
+    drag[...] = drags * (2.0 / SAMPLES)
+    stiff[...] = stiffs
+    strength = wets * stiff[...]
+    packed = jnp.sum(
+        columns_to_lanes(strength[:, 0:1], 64) + columns_to_lanes(strength[:, LANES - 1:LANES], 96), axis=0, keepdims=True
+    )
+    friction()
     local_terms(0, 0, ROWS)
     loads[3].wait()
     local_residual(0, 0, ROWS)

time: 61.9 us -> 62 us (level)
  no operation moved by 1% of the time
where the time goes in v5:
time: 62 us; the launch traced here: 61.8 us
  Pallas kernels  61.1 us (99%)
  local copies, waits for them, and re-layouts  0.71 us (1%)
    pallas_call x1, Pallas kernels, body(): pl.pallas_call(kernel, out_shape=pltpu.VMEM(flat, f32), in_specs=[any_spe...  61.1 us

profile of v5, /device:TPU:1, one launch (start us, length us, event | category | flops | bytes accessed | tf_op | source)
XLA Modules:
  0.0 61.8 jit_solution(4485552751206106621)
XLA Ops:
  0.0 61.1 %shard_map.91 = f32[512,128]{1,0:T(8,128)S(1)} custom-call(f32[512,128]{1,0:T(8,128)} %bitcast.4, f32[512,128]{1,0:T(8,128)} %bitcast.5, s32[32,128]{1,0:T(8,128)} %wet_hbm.1, s32[32,128]{1,0:T(8,128)} %band_hbm.1, f32[8]{0:T(128)} %drag_ref.1, f32[8]{0:T(128)} %stiff_ref.1, f32[48]{0:T(128)} %times_ref.1, f32[8,128,128]{2,1,0:T(8,128)} %zonal_hbm.1, ...), custom_call_target="tpu_custom_call" | custom-call | flops 600000000 | bytes 2500000 | tf_op jit(solution)/shard_map/pallas_call | solution.py:469
  61.1 0.7 %copy.11 = f32[8,2,32,128]{3,2,1,0:T(8,128)} copy(f32[8,2,32,128]{3,2,1,0:T(8,128)S(1)} %bitcast.3) | data formatting | bytes 524288

commit v6 on v3

--- a/solution.py
+++ b/solution.py
@@ -442,16 +442,19 @@
         for half in range(2):
             await_half(half, peer, fwd_out.at[1], fwd_in.at[1], fwd_send.at[1], fwd_recv.at[1], place)
         edge_terms(peer, 1)
-    pending.extend(solve(1))
+    leaving = solve(1)
+    for copy in pending:
+        copy.wait_send()
     for half in range(2):
+        if half == 1:
+            for copy in leaving:
+                copy.wait_send()
         for peer in peers:
             await_half(half, peer, *returns(1))
         for c in range(COMPS):
             rows = pl.ds(c * ROWS + half * HALF, HALF)
             state = cur[1, pl.ds(half * HALF * COMPS + c, HALF, stride=COMPS), :]
             out_ref[rows, :] = state + 0.25 * wet[half * HALF:(half + 1) * HALF] * ret_in[1, rows, :]
-    for copy in pending:
-        copy.wait_send()
 
 
 def body(

time: 61.9 us -> 61.7 us (level)
  no operation moved by 1% of the time
where the time goes in v6:
time: 61.7 us; the launch traced here: 61.5 us
  Pallas kernels  60.8 us (99%)
  local copies, waits for them, and re-layouts  0.71 us (1%)
    pallas_call x1, Pallas kernels, body(): pl.pallas_call(kernel, out_shape=pltpu.VMEM(flat, f32), in_specs=[any_spe...  60.8 us

profile of v6, /device:TPU:1, one launch (start us, length us, event | category | flops | bytes accessed | tf_op | source)
XLA Modules:
  0.0 61.5 jit_solution(7150258857449330661)
XLA Ops:
  0.0 60.8 %shard_map.91 = f32[512,128]{1,0:T(8,128)S(1)} custom-call(f32[512,128]{1,0:T(8,128)} %bitcast.4, f32[512,128]{1,0:T(8,128)} %bitcast.5, s32[32,128]{1,0:T(8,128)} %wet_hbm.1, s32[32,128]{1,0:T(8,128)} %band_hbm.1, f32[8]{0:T(128)} %drag_ref.1, f32[8]{0:T(128)} %stiff_ref.1, f32[48]{0:T(128)} %times_ref.1, f32[8,128,128]{2,1,0:T(8,128)} %zonal_hbm.1, ...), custom_call_target="tpu_custom_call" | custom-call | flops 600000000 | bytes 2500000 | tf_op jit(solution)/shard_map/pallas_call | solution.py:476
  60.8 0.7 %copy.11 = f32[8,2,32,128]{3,2,1,0:T(8,128)} copy(f32[8,2,32,128]{3,2,1,0:T(8,128)S(1)} %bitcast.3) | data formatting | bytes 524288

commit v7 on v6

--- a/solution.py
+++ b/solution.py
@@ -339,7 +339,7 @@
     friction()
     pl.semaphore_wait(barrier, 5 + len(peers))
     halos = []
-    for slot, device in ((2, east), (3, west), (0, south), (1, north)):
+    for slot, device in ((0, south), (1, north), (2, east), (3, west)):
         copy = remote(halo_out.at[slot], halo_in.at[slot], halo_send.at[slot], halo_recv.at[slot], device)
         copy.start()
         halos.append(copy)
@@ -371,7 +371,6 @@
     for j in range(2, 8):
         mid_out[pl.ds(j, COMPS, stride=8), :] = jnp.zeros(tile, jnp.float32)
     mids = (mid_out, mid_in, mid_send, mid_recv, 8)
-    pending.extend(exchange(*mids))
 
     loads[4].wait()
     loads[5].wait()
@@ -396,6 +395,7 @@
     for owner in range(RANKS):
         edge_terms(owner, 0)
     pending.extend(solve(0))
+    pending.extend(exchange(*mids))
 
     for owner in range(RANKS):
         value = jnp.concatenate([ret_out[0, solved_rows(0, owner), :], ret_out[0, solved_rows(1, owner), :]], axis=0)

time: 61.7 us -> 62 us (level)
  no operation moved by 1% of the time
where the time goes in v7:
time: 62 us; the launch traced here: 61.8 us
  Pallas kernels  61.1 us (99%)
  local copies, waits for them, and re-layouts  0.71 us (1%)
    pallas_call x1, Pallas kernels, body(): pl.pallas_call(kernel, out_shape=pltpu.VMEM(flat, f32), in_specs=[any_spe...  61.1 us

profile of v7, /device:TPU:1, one launch (start us, length us, event | category | flops | bytes accessed | tf_op | source)
XLA Modules:
  0.0 61.8 jit_solution(1985191974088418504)
XLA Ops:
  0.0 61.1 %shard_map.91 = f32[512,128]{1,0:T(8,128)S(1)} custom-call(f32[512,128]{1,0:T(8,128)} %bitcast.4, f32[512,128]{1,0:T(8,128)} %bitcast.5, s32[32,128]{1,0:T(8,128)} %wet_hbm.1, s32[32,128]{1,0:T(8,128)} %band_hbm.1, f32[8]{0:T(128)} %drag_ref.1, f32[8]{0:T(128)} %stiff_ref.1, f32[48]{0:T(128)} %times_ref.1, f32[8,128,128]{2,1,0:T(8,128)} %zonal_hbm.1, ...), custom_call_target="tpu_custom_call" | custom-call | flops 600000000 | bytes 2500000 | tf_op jit(solution)/shard_map/pallas_call | solution.py:476
  61.1 0.7 %copy.11 = f32[8,2,32,128]{3,2,1,0:T(8,128)} copy(f32[8,2,32,128]{3,2,1,0:T(8,128)S(1)} %bitcast.3) | data formatting | bytes 524288
